TPU v7x, 512 devices: a whole 4x4x16 slice. The times are simulated.
512 devices in a mesh: leaf: 64 (over z, y), sec: 8 (over x, core).
Axes of the slice: x: 4, y: 4, z: 16, core: 2. Of those that a mesh axis runs over, the one named last changes fastest.
Arguments:
- leaf_inv: bfloat16 [524288, 1024], P(('leaf', 'sec')), may hold values from -0.1875 to 0.1875
- subtree_blocks: int32 [64, 8], P('leaf', 'sec'), may hold values from 1 to 8
- subtree_shift_rhs: bfloat16 [524288, 128], P(('leaf', 'sec')), may hold values from -6 to 6
- leaf_noise: bfloat16 [524288, 128], P(('leaf', 'sec')), may hold values from -6 to 6
- leaf_dev: bfloat16 [524288], P(('leaf', 'sec')), may hold values from 0.29882812 to 3
- sep_inv: bfloat16 [16384, 3584], P(('leaf', 'sec')), may hold values from -0.1875 to 0.1875
- sep_panel: bfloat16 [16384, 3584], P(('leaf', 'sec')), may hold values from -0.1875 to 0.1875
- sep_rhs: bfloat16 [3, 16384, 128], P(None, ('leaf', 'sec')), may hold values from -6 to 6
- sep_noise: bfloat16 [3, 16384, 128], P(None, ('leaf', 'sec')), may hold values from -6 to 6
- sep_dev: bfloat16 [3, 16384], P(None, ('leaf', 'sec')), may hold values from 0.29882812 to 3
Outputs:
- subtree_scaled_samples: bfloat16 [524288, 128], P(('leaf', 'sec'))
- sep_sample: bfloat16 [3, 16384, 128], P(None, ('leaf', 'sec'))
All inputs are finite; a program needn't handle non-finite values.
Results may differ from a plain program's by a relative error of at most 0.019.
Values may be sent and summed in bfloat16 or wider, within the bound.
A program may use at most 64 MiB of HBM per device.

v0:
```python
import jax
import jax.numpy as jnp
from jax import lax
from jax.sharding import PartitionSpec as P

BLOCK = 128


def from_partner(block, axis, apart):
    count = lax.axis_size(axis)
    route = []
    for low in range(count):
        high = low | 1 << apart
        if high != low and high < count:
            route += [(low, high), (high, low)]
    return lax.ppermute(block, axis, route)


def pair_gather(block, height):
    leaf_place = lax.axis_index("leaf")
    for bit_index in range(height):
        partner = from_partner(block, "leaf", bit_index)
        upper_half = leaf_place >> bit_index & 1 == 1
        block = jnp.where(
            upper_half, jnp.concatenate([partner, block], 0), jnp.concatenate([block, partner], 0)
        )
    return block


def group_gather(piece, height):
    block = lax.all_gather(piece, "sec", axis=0, tiled=True)
    return pair_gather(block, height)


def halve_pairs(partial_sum, height):
    leaf_place = lax.axis_index("leaf")
    for bit_index in reversed(range(height)):
        half_rows = partial_sum.shape[0] // 2
        lower_rows = partial_sum[:half_rows]
        upper_rows = partial_sum[half_rows:]
        upper_half = leaf_place >> bit_index & 1 == 1
        kept = jnp.where(upper_half, upper_rows, lower_rows)
        outgoing = jnp.where(upper_half, lower_rows, upper_rows)
        partial_sum = kept + from_partner(outgoing, "leaf", bit_index)
    return partial_sum


def group_reduce(partial_sum, height):
    reduced = halve_pairs(partial_sum, height)
    return lax.psum_scatter(reduced, "sec", scatter_dimension=0, tiled=True)


def transposed_product(matrix, vector):
    return lax.dot_general(
        matrix, vector, (((0,), (0,)), ((), ())), preferred_element_type=jnp.float32
    )


def on_device(
    leaf_inv,
    subtree_blocks,
    subtree_shift_rhs,
    leaf_noise,
    leaf_dev,
    sep_inv,
    sep_panel,
    sep_rhs,
    sep_noise,
    sep_dev,
):
    subtree_row_count = leaf_inv.shape[0]
    row_count = sep_inv.shape[0]
    levels = sep_rhs.shape[0]
    sections = lax.axis_size("sec")
    active_rows = subtree_blocks[0, 0] * BLOCK
    row_positions = jnp.arange(subtree_row_count, dtype=jnp.int32)
    row_activity = (row_positions >= subtree_row_count - active_rows)[:, None]
    subtree_shifted = jnp.where(
        row_activity, subtree_shift_rhs, jnp.zeros((), subtree_shift_rhs.dtype)
    )
    forward_subtree = jnp.dot(leaf_inv, subtree_shifted, preferred_element_type=jnp.float32)
    subtree_forward_solution = jnp.where(row_activity, forward_subtree, jnp.float32(0.0)).astype(
        jnp.bfloat16
    )
    top = subtree_forward_solution[subtree_row_count - row_count :]
    solved = []
    for height in range(1, levels + 1):
        span = 2**height * sections * row_count
        offset = (2**height - 2) * sections * row_count
        children = group_gather(top, height)
        panel = sep_panel[:, offset : offset + span]
        inverse_block = sep_inv[:, offset : offset + span]
        reduced = (
            sep_rhs[height - 1].astype(jnp.float32)
            - jnp.dot(panel, children, preferred_element_type=jnp.float32)
        ).astype(jnp.bfloat16)
        whole_reduced = group_gather(reduced, height)
        result = jnp.dot(inverse_block, whole_reduced, preferred_element_type=jnp.float32).astype(
            jnp.bfloat16
        )
        solved.append(result)
        top = result
    samples = [None] * levels
    correction = None
    for height in range(levels, 0, -1):
        span = 2**height * sections * row_count
        offset = (2**height - 2) * sections * row_count
        panel = sep_panel[:, offset : offset + span]
        inverse_block = sep_inv[:, offset : offset + span]
        summed = solved[height - 1].astype(jnp.float32) + sep_noise[height - 1].astype(jnp.float32)
        if correction is not None:
            summed = summed - correction
        vector = summed.astype(jnp.bfloat16)
        backed = group_reduce(transposed_product(inverse_block, vector), height).astype(
            jnp.bfloat16
        )
        samples[height - 1] = (
            sep_dev[height - 1][:, None].astype(jnp.float32) * backed.astype(jnp.float32)
        ).astype(jnp.bfloat16)
        correction = group_reduce(transposed_product(panel, backed), height)
    leading = jnp.zeros((subtree_row_count - row_count, correction.shape[1]), jnp.float32)
    placed = jnp.concatenate([leading, correction], axis=0)
    subtree_summed = (
        subtree_forward_solution.astype(jnp.float32) + leaf_noise.astype(jnp.float32) - placed
    )
    subtree_weight = jnp.where(row_activity, subtree_summed, jnp.float32(0.0)).astype(jnp.bfloat16)
    subtree_solution = transposed_product(leaf_inv, subtree_weight)
    sample_scales = leaf_dev[:, None].astype(jnp.float32)
    subtree_scaled_samples = jnp.where(
        row_activity, sample_scales * subtree_solution, jnp.float32(0.0)
    ).astype(jnp.bfloat16)
    return (subtree_scaled_samples, jnp.stack(samples))


def solution(mesh):
    in_specs = (
        P(("leaf", "sec"), None),
        P("leaf", "sec"),
        P(("leaf", "sec"), None),
        P(("leaf", "sec"), None),
        P(("leaf", "sec")),
        P(("leaf", "sec"), None),
        P(("leaf", "sec"), None),
        P(None, ("leaf", "sec"), None),
        P(None, ("leaf", "sec"), None),
        P(None, ("leaf", "sec")),
    )
    out_specs = (P(("leaf", "sec"), None), P(None, ("leaf", "sec"), None))
    return jax.shard_map(
        on_device, mesh=mesh, in_specs=in_specs, out_specs=out_specs, check_vma=False
    )
```

profile of v0, /device:TPU:8, one launch (start us, length us, event | category | flops | bytes accessed | tf_op | source)
XLA Modules:
  0.0 543.7 jit_solution(11738488947053809435)
XLA Ops:
  10.1 13.1 %all_gather.18 = bf16[256,128]{1,0:T(8,128)(2,1)S(1)} all-gather(bf16[32,128]{1,0:T(8,128)(2,1)S(1)} %copy.28), channel_id=1, replica_groups=mesh['leaf'=64,'sec'=8] {'sec'}, dimensions={0}, use_global_device_ids=true | all-gather | bytes 73728 | tf_op jit(solution)/shard_map/all_gather | solution.py:31
  23.3 7.4 %collective-permute-start = (bf16[256,128]{1,0:T(8,128)(2,1)S(1)}, bf16[256,128]{1,0:T(8,128)(2,1)S(1)}, u32[]{:S(2)}, u32[]{:S(2)}) collective-permute-start(bf16[256,128]{1,0:T(8,128)(2,1)S(1)} %all_gather.18), channel_id=1, source_target_pairs={{0,8},{8,0},{16,24},{24,16},{32,40},{40,32},{48,56},{56,48},{64,72... | collective-permute-start | bytes 196616 | tf_op jit(solution)/shard_map/ppermute | solution.py:16
  33.3 12.7 %all_gather.19 = bf16[256,128]{1,0:T(8,128)(2,1)S(1)} all-gather(bf16[32,128]{1,0:T(8,128)(2,1)S(1)} %fusion.8), channel_id=1, replica_groups=mesh['leaf'=64,'sec'=8] {'sec'}, dimensions={0}, use_global_device_ids=true | all-gather | bytes 73728 | tf_op jit(solution)/shard_map/all_gather | solution.py:31
  53.2 12.7 %all_gather.20 = bf16[256,128]{1,0:T(8,128)(2,1)S(1)} all-gather(bf16[32,128]{1,0:T(8,128)(2,1)S(1)} %fusion.15), channel_id=1, replica_groups=mesh['leaf'=64,'sec'=8] {'sec'}, dimensions={0}, use_global_device_ids=true | all-gather | bytes 73728 | tf_op jit(solution)/shard_map/all_gather | solution.py:31
  74.1 6.4 %collective-permute-done.3 = bf16[512,128]{1,0:T(8,128)(2,1)S(1)} collective-permute-done((bf16[512,128]{1,0:T(8,128)(2,1)S(1)}, bf16[512,128]{1,0:T(8,128)(2,1)S(1)}, u32[]{:S(2)}, u32[]{:S(2)}) %collective-permute-start.3) | collective-permute-done | bytes 131104 | tf_op jit(solution)/shard_map/ppermute | solution.py:16
  80.7 12.8 %all_gather.21 = bf16[256,128]{1,0:T(8,128)(2,1)S(1)} all-gather(bf16[32,128]{1,0:T(8,128)(2,1)S(1)} %fusion.9), channel_id=1, replica_groups=mesh['leaf'=64,'sec'=8] {'sec'}, dimensions={0}, use_global_device_ids=true | all-gather | bytes 73728 | tf_op jit(solution)/shard_map/all_gather | solution.py:31
  101.9 6.2 %collective-permute-done.5 = bf16[512,128]{1,0:T(8,128)(2,1)S(1)} collective-permute-done((bf16[512,128]{1,0:T(8,128)(2,1)S(1)}, bf16[512,128]{1,0:T(8,128)(2,1)S(1)}, u32[]{:S(2)}, u32[]{:S(2)}) %collective-permute-start.5) | collective-permute-done | bytes 131104 | tf_op jit(solution)/shard_map/ppermute | solution.py:16
  109.1 12.8 %all_gather.22 = bf16[256,128]{1,0:T(8,128)(2,1)S(1)} all-gather(bf16[32,128]{1,0:T(8,128)(2,1)S(1)} %fusion.16), channel_id=1, replica_groups=mesh['leaf'=64,'sec'=8] {'sec'}, dimensions={0}, use_global_device_ids=true | all-gather | bytes 73728 | tf_op jit(solution)/shard_map/all_gather | solution.py:31
  130.3 6.2 %collective-permute-done.7 = bf16[512,128]{1,0:T(8,128)(2,1)S(1)} collective-permute-done((bf16[512,128]{1,0:T(8,128)(2,1)S(1)}, bf16[512,128]{1,0:T(8,128)(2,1)S(1)}, u32[]{:S(2)}, u32[]{:S(2)}) %collective-permute-start.7) | collective-permute-done | bytes 131104 | tf_op jit(solution)/shard_map/ppermute | solution.py:16
  138.5 6.5 %collective-permute-done.8 = bf16[1024,128]{1,0:T(8,128)(2,1)S(1)} collective-permute-done((bf16[1024,128]{1,0:T(8,128)(2,1)S(1)}, bf16[1024,128]{1,0:T(8,128)(2,1)S(1)}, u32[]{:S(2)}, u32[]{:S(2)}) %collective-permute-start.8) | collective-permute-done | bytes 262176 | tf_op jit(solution)/shard_map/ppermute | solution.py:16
  145.3 12.8 %all_gather.23 = bf16[256,128]{1,0:T(8,128)(2,1)S(1)} all-gather(bf16[32,128]{1,0:T(8,128)(2,1)S(1)} %fusion.10), channel_id=1, replica_groups=mesh['leaf'=64,'sec'=8] {'sec'}, dimensions={0}, use_global_device_ids=true | all-gather | bytes 73728 | tf_op jit(solution)/shard_map/all_gather | solution.py:31
  166.5 6.2 %collective-permute-done.10 = bf16[512,128]{1,0:T(8,128)(2,1)S(1)} collective-permute-done((bf16[512,128]{1,0:T(8,128)(2,1)S(1)}, bf16[512,128]{1,0:T(8,128)(2,1)S(1)}, u32[]{:S(2)}, u32[]{:S(2)}) %collective-permute-start.10) | collective-permute-done | bytes 131104 | tf_op jit(solution)/shard_map/ppermute | solution.py:16
  175.0 6.4 %collective-permute-done.11 = bf16[1024,128]{1,0:T(8,128)(2,1)} collective-permute-done((bf16[1024,128]{1,0:T(8,128)(2,1)S(1)}, bf16[1024,128]{1,0:T(8,128)(2,1)}, u32[]{:S(2)}, u32[]{:S(2)}) %collective-permute-start.11) | collective-permute-done | bytes 262176 | tf_op jit(solution)/shard_map/ppermute | solution.py:16
  185.5 11.0 %collective-permute-done.12 = f32[1024,128]{0,1:T(8,128)S(1)} collective-permute-done((f32[1024,128]{0,1:T(8,128)S(1)}, f32[1024,128]{0,1:T(8,128)S(1)}, u32[]{:S(2)}, u32[]{:S(2)}) %collective-permute-start.12) | collective-permute-done | bytes 524320 | tf_op jit(solution)/shard_map/ppermute | solution.py:16
  198.9 8.2 %collective-permute-done.13 = f32[512,128]{0,1:T(8,128)S(1)} collective-permute-done((f32[512,128]{0,1:T(8,128)S(1)}, f32[512,128]{0,1:T(8,128)S(1)}, u32[]{:S(2)}, u32[]{:S(2)}) %collective-permute-start.13) | collective-permute-done | bytes 262176 | tf_op jit(solution)/shard_map/ppermute | solution.py:16
  214.9 37.6 %reduce-scatter.19.cloned.1.call-done = f32[32,128]{1,0:T(8,128)} async-done(((f32[256,128]{1,0:T(8,128)}), f32[32,128]{1,0:T(8,128)}) %reduce-scatter.19.cloned.1.call-update) | async-done | bytes 16400
  257.3 9.5 %collective-permute-done.15 = f32[1024,128]{0,1:T(8,128)S(1)} collective-permute-done((f32[1024,128]{0,1:T(8,128)S(1)}, f32[1024,128]{0,1:T(8,128)S(1)}, u32[]{:S(2)}, u32[]{:S(2)}) %collective-permute-start.15) | collective-permute-done | bytes 524320 | tf_op jit(solution)/shard_map/ppermute | solution.py:16
  271.0 5.7 %collective-permute-done.16 = f32[512,128]{0,1:T(8,128)S(1)} collective-permute-done((f32[512,128]{0,1:T(8,128)S(1)}, f32[512,128]{0,1:T(8,128)S(1)}, u32[]{:S(2)}, u32[]{:S(2)}) %collective-permute-start.16) | collective-permute-done | bytes 262176 | tf_op jit(solution)/shard_map/ppermute | solution.py:16
  284.5 41.8 %reduce-scatter.21.cloned.1.call-done = f32[32,128]{1,0:T(8,128)} async-done(((f32[256,128]{1,0:T(8,128)}), f32[32,128]{1,0:T(8,128)}) %reduce-scatter.21.cloned.1.call-update) | async-done | bytes 16400 | tf_op jit(solution)/shard_map/reduce_scatter | solution.py:50
  331.4 5.8 %collective-permute-done.18 = f32[512,128]{0,1:T(8,128)S(1)} collective-permute-done((f32[512,128]{0,1:T(8,128)S(1)}, f32[512,128]{0,1:T(8,128)S(1)}, u32[]{:S(2)}, u32[]{:S(2)}) %collective-permute-start.18) | collective-permute-done | bytes 262176 | tf_op jit(solution)/shard_map/ppermute | solution.py:16
  344.9 39.3 %reduce-scatter.23.cloned.1.call-done = f32[32,128]{1,0:T(8,128)} async-done(((f32[256,128]{1,0:T(8,128)}), f32[32,128]{1,0:T(8,128)}) %reduce-scatter.23.cloned.1.call-update) | async-done | bytes 16400
  403.1 39.4 %reduce-scatter.25.cloned.1.call-done = f32[32,128]{1,0:T(8,128)} async-done(((f32[256,128]{1,0:T(8,128)}), f32[32,128]{1,0:T(8,128)}) %reduce-scatter.25.cloned.1.call-update) | async-done | bytes 16400 | tf_op jit(solution)/shard_map/reduce_scatter | solution.py:50
  451.5 37.2 %reduce-scatter.27.cloned.1.call-done = f32[32,128]{1,0:T(8,128)} async-done(((f32[256,128]{1,0:T(8,128)}), f32[32,128]{1,0:T(8,128)}) %reduce-scatter.27.cloned.1.call-update) | async-done | bytes 16400
  498.1 36.7 %reduce-scatter.29.cloned.1.call-done = f32[32,128]{1,0:T(8,128)} async-done(((f32[256,128]{1,0:T(8,128)}), f32[32,128]{1,0:T(8,128)}) %reduce-scatter.29.cloned.1.call-update) | async-done | bytes 16400
  (134 shorter events, 134.1 us)
Async XLA Ops:
  7.2 245.3 %reduce-scatter.19.cloned.1.call-start = ((), (), s32[]{:S(2)}) async-start(), calls=%async_computation.6 | async-start | bytes 147456
  23.3 9.9 %collective-permute-start = (bf16[256,128]{1,0:T(8,128)(2,1)S(1)}, bf16[256,128]{1,0:T(8,128)(2,1)S(1)}, u32[]{:S(2)}, u32[]{:S(2)}) collective-permute-start(bf16[256,128]{1,0:T(8,128)(2,1)S(1)} %all_gather.18), channel_id=1, source_target_pairs={{0,8},{8,0},{16,24},{24,16},{32,40},{40,32},{48,56},{56,48},{64,72... | collective-permute-start | bytes 196616 | tf_op jit(solution)/shard_map/ppermute | solution.py:16
  72.2 8.4 %collective-permute-start.3 = (bf16[512,128]{1,0:T(8,128)(2,1)S(1)}, bf16[512,128]{1,0:T(8,128)(2,1)S(1)}, u32[]{:S(2)}, u32[]{:S(2)}) collective-permute-start(bf16[512,128]{1,0:T(8,128)(2,1)S(1)} %maximum_select_fusion.15), channel_id=1, source_target_pairs={{0,16},{16,0},{8,24},{24,8},{32,48},{48,32},{40,56},{56,40},{64,80... | collective-permute-start | bytes 393224 | tf_op jit(solution)/shard_map/ppermute | solution.py:16
  99.7 8.4 %collective-permute-start.5 = (bf16[512,128]{1,0:T(8,128)(2,1)S(1)}, bf16[512,128]{1,0:T(8,128)(2,1)S(1)}, u32[]{:S(2)}, u32[]{:S(2)}) collective-permute-start(bf16[512,128]{1,0:T(8,128)(2,1)S(1)} %maximum_select_fusion.16), channel_id=1, source_target_pairs={{0,16},{16,0},{8,24},{24,8},{32,48},{48,32},{40,56},{56,40},{64,80... | collective-permute-start | bytes 393224 | tf_op jit(solution)/shard_map/ppermute | solution.py:16
  128.1 8.4 %collective-permute-start.7 = (bf16[512,128]{1,0:T(8,128)(2,1)S(1)}, bf16[512,128]{1,0:T(8,128)(2,1)S(1)}, u32[]{:S(2)}, u32[]{:S(2)}) collective-permute-start(bf16[512,128]{1,0:T(8,128)(2,1)S(1)} %maximum_select_fusion.17), channel_id=1, source_target_pairs={{0,16},{16,0},{8,24},{24,8},{32,48},{48,32},{40,56},{56,40},{64,80... | collective-permute-start | bytes 393224 | tf_op jit(solution)/shard_map/ppermute | solution.py:16
  136.6 8.5 %collective-permute-start.8 = (bf16[1024,128]{1,0:T(8,128)(2,1)S(1)}, bf16[1024,128]{1,0:T(8,128)(2,1)S(1)}, u32[]{:S(2)}, u32[]{:S(2)}) collective-permute-start(bf16[1024,128]{1,0:T(8,128)(2,1)S(1)} %maximum_select_fusion.9), channel_id=1, source_target_pairs={{0,32},{32,0},{8,40},{40,8},{16,48},{48,16},{24,56},{56,24},{64,96... | collective-permute-start | bytes 786440 | tf_op jit(solution)/shard_map/ppermute | solution.py:16
  164.3 8.4 %collective-permute-start.10 = (bf16[512,128]{1,0:T(8,128)(2,1)S(1)}, bf16[512,128]{1,0:T(8,128)(2,1)S(1)}, u32[]{:S(2)}, u32[]{:S(2)}) collective-permute-start(bf16[512,128]{1,0:T(8,128)(2,1)S(1)} %maximum_select_fusion.18), channel_id=1, source_target_pairs={{0,16},{16,0},{8,24},{24,8},{32,48},{48,32},{40,56},{56,40},{64,80... | collective-permute-start | bytes 393224 | tf_op jit(solution)/shard_map/ppermute | solution.py:16
  172.7 8.6 %collective-permute-start.11 = (bf16[1024,128]{1,0:T(8,128)(2,1)S(1)}, bf16[1024,128]{1,0:T(8,128)(2,1)}, u32[]{:S(2)}, u32[]{:S(2)}) collective-permute-start(bf16[1024,128]{1,0:T(8,128)(2,1)S(1)} %maximum_select_fusion.10), channel_id=1, source_target_pairs={{0,32},{32,0},{8,40},{40,8},{16,48},{48,16},{24,56},{56,24},{64,96... | collective-permute-start | bytes 786440 | tf_op jit(solution)/shard_map/ppermute | solution.py:16
  183.3 13.2 %collective-permute-start.12 = (f32[1024,128]{0,1:T(8,128)S(1)}, f32[1024,128]{0,1:T(8,128)S(1)}, u32[]{:S(2)}, u32[]{:S(2)}) collective-permute-start(f32[1024,128]{0,1:T(8,128)S(1)} %slice_select_fusion.1), channel_id=1, source_target_pairs={{0,32},{32,0},{8,40},{40,8},{16,48},{48,16},{24,56},{56,24},{64,96... | collective-permute-start | bytes 1572872 | tf_op jit(solution)/shard_map/ppermute | solution.py:16
  196.6 10.5 %collective-permute-start.13 = (f32[512,128]{0,1:T(8,128)S(1)}, f32[512,128]{0,1:T(8,128)S(1)}, u32[]{:S(2)}, u32[]{:S(2)}) collective-permute-start(f32[512,128]{0,1:T(8,128)S(1)} %slice_select_fusion.5), channel_id=1, source_target_pairs={{0,16},{16,0},{8,24},{24,8},{32,48},{48,32},{40,56},{56,40},{64,80... | collective-permute-start | bytes 786440 | tf_op jit(solution)/shard_map/ppermute | solution.py:16
  207.2 6.9 %collective-permute-start.14 = (f32[256,128]{0,1:T(8,128)S(1)}, f32[256,128]{0,1:T(8,128)S(1)}, u32[]{:S(2)}, u32[]{:S(2)}) collective-permute-start(f32[256,128]{0,1:T(8,128)S(1)} %slice_select_fusion.11), channel_id=1, source_target_pairs={{0,8},{8,0},{16,24},{24,16},{32,40},{40,32},{48,56},{56,48},{64,72... | collective-permute-start | bytes 393224 | tf_op jit(solution)/shard_map/ppermute | solution.py:16
  214.8 111.4 %reduce-scatter.21.cloned.1.call-start = ((), (), s32[]{:S(2)}) async-start(), calls=%async_computation.7 | async-start | bytes 147456 | tf_op jit(solution)/shard_map/reduce_scatter | solution.py:50
  253.7 13.1 %collective-permute-start.15 = (f32[1024,128]{0,1:T(8,128)S(1)}, f32[1024,128]{0,1:T(8,128)S(1)}, u32[]{:S(2)}, u32[]{:S(2)}) collective-permute-start(f32[1024,128]{0,1:T(8,128)S(1)} %slice_select_fusion), channel_id=1, source_target_pairs={{0,32},{32,0},{8,40},{40,8},{16,48},{48,16},{24,56},{56,24},{64,96... | collective-permute-start | bytes 1572872 | tf_op jit(solution)/shard_map/ppermute | solution.py:16
  266.9 9.8 %collective-permute-start.16 = (f32[512,128]{0,1:T(8,128)S(1)}, f32[512,128]{0,1:T(8,128)S(1)}, u32[]{:S(2)}, u32[]{:S(2)}) collective-permute-start(f32[512,128]{0,1:T(8,128)S(1)} %slice_select_fusion.4), channel_id=1, source_target_pairs={{0,16},{16,0},{8,24},{24,8},{32,48},{48,32},{40,56},{56,40},{64,80... | collective-permute-start | bytes 786440 | tf_op jit(solution)/shard_map/ppermute | solution.py:16
  276.7 6.9 %collective-permute-start.17 = (f32[256,128]{0,1:T(8,128)S(1)}, f32[256,128]{0,1:T(8,128)S(1)}, u32[]{:S(2)}, u32[]{:S(2)}) collective-permute-start(f32[256,128]{0,1:T(8,128)S(1)} %slice_select_fusion.10), channel_id=1, source_target_pairs={{0,8},{8,0},{16,24},{24,16},{32,40},{40,32},{48,56},{56,48},{64,72... | collective-permute-start | bytes 393224 | tf_op jit(solution)/shard_map/ppermute | solution.py:16
  284.4 99.9 %reduce-scatter.23.cloned.1.call-start = ((), (), s32[]{:S(2)}) async-start(), calls=%async_computation.8 | async-start | bytes 147456
  327.4 9.8 %collective-permute-start.18 = (f32[512,128]{0,1:T(8,128)S(1)}, f32[512,128]{0,1:T(8,128)S(1)}, u32[]{:S(2)}, u32[]{:S(2)}) collective-permute-start(f32[512,128]{0,1:T(8,128)S(1)} %slice_select_fusion.3), channel_id=1, source_target_pairs={{0,16},{16,0},{8,24},{24,8},{32,48},{48,32},{40,56},{56,40},{64,80... | collective-permute-start | bytes 786440 | tf_op jit(solution)/shard_map/ppermute | solution.py:16
  337.2 6.9 %collective-permute-start.19 = (f32[256,128]{0,1:T(8,128)S(1)}, f32[256,128]{0,1:T(8,128)S(1)}, u32[]{:S(2)}, u32[]{:S(2)}) collective-permute-start(f32[256,128]{0,1:T(8,128)S(1)} %slice_select_fusion.9), channel_id=1, source_target_pairs={{0,8},{8,0},{16,24},{24,16},{32,40},{40,32},{48,56},{56,48},{64,72... | collective-permute-start | bytes 393224 | tf_op jit(solution)/shard_map/ppermute | solution.py:16
  344.9 97.6 %reduce-scatter.25.cloned.1.call-start = ((), (), s32[]{:S(2)}) async-start(), calls=%async_computation.9 | async-start | bytes 147456 | tf_op jit(solution)/shard_map/reduce_scatter | solution.py:50
  385.4 9.9 %collective-permute-start.20 = (f32[512,128]{0,1:T(8,128)S(1)}, f32[512,128]{0,1:T(8,128)S(1)}, u32[]{:S(2)}, u32[]{:S(2)}) collective-permute-start(f32[512,128]{0,1:T(8,128)S(1)} %slice_select_fusion.2), channel_id=1, source_target_pairs={{0,16},{16,0},{8,24},{24,8},{32,48},{48,32},{40,56},{56,40},{64,80... | collective-permute-start | bytes 786440 | tf_op jit(solution)/shard_map/ppermute | solution.py:16
  395.4 6.9 %collective-permute-start.21 = (f32[256,128]{0,1:T(8,128)S(1)}, f32[256,128]{0,1:T(8,128)S(1)}, u32[]{:S(2)}, u32[]{:S(2)}) collective-permute-start(f32[256,128]{0,1:T(8,128)S(1)} %slice_select_fusion.8), channel_id=1, source_target_pairs={{0,8},{8,0},{16,24},{24,16},{32,40},{40,32},{48,56},{56,48},{64,72... | collective-permute-start | bytes 393224 | tf_op jit(solution)/shard_map/ppermute | solution.py:16
  403.0 85.7 %reduce-scatter.27.cloned.1.call-start = ((), (), s32[]{:S(2)}) async-start(), calls=%async_computation.10 | async-start | bytes 147456
  443.5 6.9 %collective-permute-start.22 = (f32[256,128]{0,1:T(8,128)S(1)}, f32[256,128]{0,1:T(8,128)S(1)}, u32[]{:S(2)}, u32[]{:S(2)}) collective-permute-start(f32[256,128]{0,1:T(8,128)S(1)} %slice_select_fusion.7), channel_id=1, source_target_pairs={{0,8},{8,0},{16,24},{24,16},{32,40},{40,32},{48,56},{56,48},{64,72... | collective-permute-start | bytes 393224 | tf_op jit(solution)/shard_map/ppermute | solution.py:16
  451.2 83.6 %reduce-scatter.29.cloned.1.call-start = ((), (), s32[]{:S(2)}) async-start(), calls=%async_computation.11 | async-start | bytes 147456
  (15 other events, 421.1 us)
Sparse Core Ops, SparseCore 0:
  215.0 37.4 reduce-scatter.18
  284.5 41.6 reduce-scatter.20
  345.0 39.2 reduce-scatter.22
  403.1 39.3 reduce-scatter.24
  451.3 37.3 reduce-scatter.26
  497.5 37.2 reduce-scatter.28
where the time goes:
time: 545 us; the launch traced here: 544 us
  waiting for transfers between devices  355 us (65%)
  blocking collectives  76.8 us (14%)
  starting transfers between devices  76.1 us (14%)
  between operations  15.5 us (3%)
  local copies, waits for them, and re-layouts  10.3 us (2%)
  matrix products  8.35 us (2%)
    unnamed x10, waiting for transfers between devices  151 us
    ppermute x24, waiting for transfers between devices, from_partner(): return lax.ppermute(block, axis, route)  123 us
    reduce_scatter x2, waiting for transfers between devices, group_reduce(): return lax.psum_scatter(reduced, 'sec', scatter_dimension=0, tiled=True)  81.2 us
    all_gather x6, blocking collectives, group_gather(): block = lax.all_gather(piece, 'sec', axis=0, tiled=True)  76.8 us
    ppermute x24, starting transfers between devices, from_partner(): return lax.ppermute(block, axis, route)  75.9 us
  transfers between devices with their start and end apart: 30, of which 30 were waited for; matrix products, arithmetic and copies ran while one was open for 0% of the time, Pallas kernels for 0%

commit v1 on v0

--- a/solution.py
+++ b/solution.py
@@ -28,7 +28,8 @@
 
 
 def group_gather(piece, height):
-    block = lax.all_gather(piece, "sec", axis=0, tiled=True)
+    sent = jnp.stack([piece] * lax.axis_size("sec"))
+    block = jnp.concatenate(lax.all_to_all(sent, "sec", 0, 0), axis=0)
     return pair_gather(block, height)
 
 

time: 545 us -> 516 us (0.947)
  the two profiles are of different devices: /device:TPU:8 before, /device:TPU:16 now
where the time goes in v1:
time: 516 us; the launch traced here: 514 us
  waiting for transfers between devices  343 us (66%)
  starting transfers between devices  85.7 us (17%)
  blocking collectives  49.7 us (10%)
  between operations  15.6 us (3%)
  local copies, waits for them, and re-layouts  10.4 us (2%)
  matrix products  8.36 us (2%)
    unnamed x10, waiting for transfers between devices  154 us
    ppermute x24, waiting for transfers between devices, from_partner(): return lax.ppermute(block, axis, route)  108 us
    ppermute x24, starting transfers between devices, from_partner(): return lax.ppermute(block, axis, route)  85.4 us
    reduce_scatter x2, waiting for transfers between devices, group_reduce(): return lax.psum_scatter(reduced, 'sec', scatter_dimension=0, tiled=True)  81 us
    all_to_all x6, blocking collectives, group_gather(): block = jnp.concatenate(lax.all_to_all(sent, 'sec', 0, 0), axis=0)  49.7 us
  transfers between devices with their start and end apart: 30, of which 30 were waited for; matrix products, arithmetic and copies ran while one was open for 0% of the time, Pallas kernels for 0%

profile of v1, /device:TPU:16, one launch (start us, length us, event | category | flops | bytes accessed | tf_op | source)
XLA Modules:
  0.0 514.4 jit_solution(8659630714993320025)
XLA Ops:
  10.2 9.7 %all_to_all.30 = bf16[8,32,128]{2,1,0:T(8,128)(2,1)S(1)} all-to-all(bf16[8,32,128]{2,1,0:T(8,128)(2,1)S(1)} %stack.20), channel_id=1, replica_groups=mesh['leaf'=64,'sec'=8] {'sec'}, dimensions={0} | all-to-all | bytes 131072 | tf_op jit(solution)/shard_map/all_to_all | solution.py:32
  26.2 8.0 %all_to_all.31 = bf16[8,32,128]{2,1,0:T(8,128)(2,1)S(1)} all-to-all(bf16[8,32,128]{2,1,0:T(8,128)(2,1)S(1)} %stack.21), channel_id=1, replica_groups=mesh['leaf'=64,'sec'=8] {'sec'}, dimensions={0} | all-to-all | bytes 131072 | tf_op jit(solution)/shard_map/all_to_all | solution.py:32
  41.3 8.0 %all_to_all.32 = bf16[8,32,128]{2,1,0:T(8,128)(2,1)S(1)} all-to-all(bf16[8,32,128]{2,1,0:T(8,128)(2,1)S(1)} %stack.22), channel_id=1, replica_groups=mesh['leaf'=64,'sec'=8] {'sec'}, dimensions={0} | all-to-all | bytes 131072 | tf_op jit(solution)/shard_map/all_to_all | solution.py:32
  55.5 5.9 %collective-permute-start.3 = (bf16[512,128]{1,0:T(8,128)(2,1)S(1)}, bf16[512,128]{1,0:T(8,128)(2,1)S(1)}, u32[]{:S(2)}, u32[]{:S(2)}) collective-permute-start(bf16[512,128]{1,0:T(8,128)(2,1)S(1)} %maximum_select_fusion.15), channel_id=1, source_target_pairs={{0,16},{16,0},{8,24},{24,8},{32,48},{48,32},{40,56},{56,40},{64,80... | collective-permute-start | bytes 393224 | tf_op jit(solution)/shard_map/ppermute | solution.py:16
  64.5 8.0 %all_to_all.33 = bf16[8,32,128]{2,1,0:T(8,128)(2,1)S(1)} all-to-all(bf16[8,32,128]{2,1,0:T(8,128)(2,1)S(1)} %stack.23), channel_id=1, replica_groups=mesh['leaf'=64,'sec'=8] {'sec'}, dimensions={0} | all-to-all | bytes 131072 | tf_op jit(solution)/shard_map/all_to_all | solution.py:32
  78.7 5.4 %collective-permute-start.5 = (bf16[512,128]{1,0:T(8,128)(2,1)S(1)}, bf16[512,128]{1,0:T(8,128)(2,1)S(1)}, u32[]{:S(2)}, u32[]{:S(2)}) collective-permute-start(bf16[512,128]{1,0:T(8,128)(2,1)S(1)} %maximum_select_fusion.16), channel_id=1, source_target_pairs={{0,16},{16,0},{8,24},{24,8},{32,48},{48,32},{40,56},{56,40},{64,80... | collective-permute-start | bytes 393224 | tf_op jit(solution)/shard_map/ppermute | solution.py:16
  88.1 8.0 %all_to_all.34 = bf16[8,32,128]{2,1,0:T(8,128)(2,1)S(1)} all-to-all(bf16[8,32,128]{2,1,0:T(8,128)(2,1)S(1)} %stack.24), channel_id=1, replica_groups=mesh['leaf'=64,'sec'=8] {'sec'}, dimensions={0} | all-to-all | bytes 131072 | tf_op jit(solution)/shard_map/all_to_all | solution.py:32
  102.3 5.4 %collective-permute-start.7 = (bf16[512,128]{1,0:T(8,128)(2,1)S(1)}, bf16[512,128]{1,0:T(8,128)(2,1)S(1)}, u32[]{:S(2)}, u32[]{:S(2)}) collective-permute-start(bf16[512,128]{1,0:T(8,128)(2,1)S(1)} %maximum_select_fusion.17), channel_id=1, source_target_pairs={{0,16},{16,0},{8,24},{24,8},{32,48},{48,32},{40,56},{56,40},{64,80... | collective-permute-start | bytes 393224 | tf_op jit(solution)/shard_map/ppermute | solution.py:16
  119.3 8.0 %all_to_all.35 = bf16[8,32,128]{2,1,0:T(8,128)(2,1)S(1)} all-to-all(bf16[8,32,128]{2,1,0:T(8,128)(2,1)S(1)} %stack.25), channel_id=1, replica_groups=mesh['leaf'=64,'sec'=8] {'sec'}, dimensions={0} | all-to-all | bytes 131072 | tf_op jit(solution)/shard_map/all_to_all | solution.py:32
  133.5 5.4 %collective-permute-start.10 = (bf16[512,128]{1,0:T(8,128)(2,1)S(1)}, bf16[512,128]{1,0:T(8,128)(2,1)S(1)}, u32[]{:S(2)}, u32[]{:S(2)}) collective-permute-start(bf16[512,128]{1,0:T(8,128)(2,1)S(1)} %maximum_select_fusion.18), channel_id=1, source_target_pairs={{0,16},{16,0},{8,24},{24,8},{32,48},{48,32},{40,56},{56,40},{64,80... | collective-permute-start | bytes 393224 | tf_op jit(solution)/shard_map/ppermute | solution.py:16
  145.3 5.0 collective-permute-done.11
  155.6 8.9 %collective-permute-done.12 = f32[1024,128]{0,1:T(8,128)S(1)} collective-permute-done((f32[1024,128]{0,1:T(8,128)S(1)}, f32[1024,128]{0,1:T(8,128)S(1)}, u32[]{:S(2)}, u32[]{:S(2)}) %collective-permute-start.12) | collective-permute-done | bytes 524320 | tf_op jit(solution)/shard_map/ppermute | solution.py:16
  164.7 5.3 %collective-permute-start.13 = (f32[512,128]{0,1:T(8,128)S(1)}, f32[512,128]{0,1:T(8,128)S(1)}, u32[]{:S(2)}, u32[]{:S(2)}) collective-permute-start(f32[512,128]{0,1:T(8,128)S(1)} %slice_select_fusion.5), channel_id=1, source_target_pairs={{0,16},{16,0},{8,24},{24,8},{32,48},{48,32},{40,56},{56,40},{64,80... | collective-permute-start | bytes 786440 | tf_op jit(solution)/shard_map/ppermute | solution.py:16
  170.0 5.3 %collective-permute-done.13 = f32[512,128]{0,1:T(8,128)S(1)} collective-permute-done((f32[512,128]{0,1:T(8,128)S(1)}, f32[512,128]{0,1:T(8,128)S(1)}, u32[]{:S(2)}, u32[]{:S(2)}) %collective-permute-start.13) | collective-permute-done | bytes 262176 | tf_op jit(solution)/shard_map/ppermute | solution.py:16
  183.1 40.4 %reduce-scatter.19.cloned.1.call-done = f32[32,128]{1,0:T(8,128)} async-done(((f32[256,128]{1,0:T(8,128)}), f32[32,128]{1,0:T(8,128)}) %reduce-scatter.19.cloned.1.call-update) | async-done | bytes 16400
  228.1 9.6 %collective-permute-done.15 = f32[1024,128]{0,1:T(8,128)S(1)} collective-permute-done((f32[1024,128]{0,1:T(8,128)S(1)}, f32[1024,128]{0,1:T(8,128)S(1)}, u32[]{:S(2)}, u32[]{:S(2)}) %collective-permute-start.15) | collective-permute-done | bytes 524320 | tf_op jit(solution)/shard_map/ppermute | solution.py:16
  241.1 6.4 %collective-permute-done.16 = f32[512,128]{0,1:T(8,128)S(1)} collective-permute-done((f32[512,128]{0,1:T(8,128)S(1)}, f32[512,128]{0,1:T(8,128)S(1)}, u32[]{:S(2)}, u32[]{:S(2)}) %collective-permute-start.16) | collective-permute-done | bytes 262176 | tf_op jit(solution)/shard_map/ppermute | solution.py:16
  255.4 41.6 %reduce-scatter.21.cloned.1.call-done = f32[32,128]{1,0:T(8,128)} async-done(((f32[256,128]{1,0:T(8,128)}), f32[32,128]{1,0:T(8,128)}) %reduce-scatter.21.cloned.1.call-update) | async-done | bytes 16400 | tf_op jit(solution)/shard_map/reduce_scatter | solution.py:51
  300.5 7.3 %collective-permute-done.18 = f32[512,128]{0,1:T(8,128)S(1)} collective-permute-done((f32[512,128]{0,1:T(8,128)S(1)}, f32[512,128]{0,1:T(8,128)S(1)}, u32[]{:S(2)}, u32[]{:S(2)}) %collective-permute-start.18) | collective-permute-done | bytes 262176 | tf_op jit(solution)/shard_map/ppermute | solution.py:16
  315.7 39.2 %reduce-scatter.23.cloned.1.call-done = f32[32,128]{1,0:T(8,128)} async-done(((f32[256,128]{1,0:T(8,128)}), f32[32,128]{1,0:T(8,128)}) %reduce-scatter.23.cloned.1.call-update) | async-done | bytes 16400
  358.6 7.3 %collective-permute-done.20 = f32[512,128]{0,1:T(8,128)S(1)} collective-permute-done((f32[512,128]{0,1:T(8,128)S(1)}, f32[512,128]{0,1:T(8,128)S(1)}, u32[]{:S(2)}, u32[]{:S(2)}) %collective-permute-start.20) | collective-permute-done | bytes 262176 | tf_op jit(solution)/shard_map/ppermute | solution.py:16
  373.7 39.4 %reduce-scatter.25.cloned.1.call-done = f32[32,128]{1,0:T(8,128)} async-done(((f32[256,128]{1,0:T(8,128)}), f32[32,128]{1,0:T(8,128)}) %reduce-scatter.25.cloned.1.call-update) | async-done | bytes 16400 | tf_op jit(solution)/shard_map/reduce_scatter | solution.py:51
  422.2 37.0 %reduce-scatter.27.cloned.1.call-done = f32[32,128]{1,0:T(8,128)} async-done(((f32[256,128]{1,0:T(8,128)}), f32[32,128]{1,0:T(8,128)}) %reduce-scatter.27.cloned.1.call-update) | async-done | bytes 16400
  468.6 36.9 %reduce-scatter.29.cloned.1.call-done = f32[32,128]{1,0:T(8,128)} async-done(((f32[256,128]{1,0:T(8,128)}), f32[32,128]{1,0:T(8,128)}) %reduce-scatter.29.cloned.1.call-update) | async-done | bytes 16400
  (140 shorter events, 137.4 us)
Async XLA Ops:
  7.2 216.2 %reduce-scatter.19.cloned.1.call-start = ((), (), s32[]{:S(2)}) async-start(), calls=%async_computation.12 | async-start | bytes 147456
  55.5 8.8 %collective-permute-start.3 = (bf16[512,128]{1,0:T(8,128)(2,1)S(1)}, bf16[512,128]{1,0:T(8,128)(2,1)S(1)}, u32[]{:S(2)}, u32[]{:S(2)}) collective-permute-start(bf16[512,128]{1,0:T(8,128)(2,1)S(1)} %maximum_select_fusion.15), channel_id=1, source_target_pairs={{0,16},{16,0},{8,24},{24,8},{32,48},{48,32},{40,56},{56,40},{64,80... | collective-permute-start | bytes 393224 | tf_op jit(solution)/shard_map/ppermute | solution.py:16
  78.7 8.4 %collective-permute-start.5 = (bf16[512,128]{1,0:T(8,128)(2,1)S(1)}, bf16[512,128]{1,0:T(8,128)(2,1)S(1)}, u32[]{:S(2)}, u32[]{:S(2)}) collective-permute-start(bf16[512,128]{1,0:T(8,128)(2,1)S(1)} %maximum_select_fusion.16), channel_id=1, source_target_pairs={{0,16},{16,0},{8,24},{24,8},{32,48},{48,32},{40,56},{56,40},{64,80... | collective-permute-start | bytes 393224 | tf_op jit(solution)/shard_map/ppermute | solution.py:16
  102.3 8.4 %collective-permute-start.7 = (bf16[512,128]{1,0:T(8,128)(2,1)S(1)}, bf16[512,128]{1,0:T(8,128)(2,1)S(1)}, u32[]{:S(2)}, u32[]{:S(2)}) collective-permute-start(bf16[512,128]{1,0:T(8,128)(2,1)S(1)} %maximum_select_fusion.17), channel_id=1, source_target_pairs={{0,16},{16,0},{8,24},{24,8},{32,48},{48,32},{40,56},{56,40},{64,80... | collective-permute-start | bytes 393224 | tf_op jit(solution)/shard_map/ppermute | solution.py:16
  110.8 8.3 %collective-permute-start.8 = (bf16[1024,128]{1,0:T(8,128)(2,1)S(1)}, bf16[1024,128]{1,0:T(8,128)(2,1)S(1)}, u32[]{:S(2)}, u32[]{:S(2)}) collective-permute-start(bf16[1024,128]{1,0:T(8,128)(2,1)S(1)} %maximum_select_fusion.9), channel_id=1, source_target_pairs={{0,32},{32,0},{8,40},{40,8},{16,48},{48,16},{24,56},{56,24},{64,96... | collective-permute-start | bytes 786440 | tf_op jit(solution)/shard_map/ppermute | solution.py:16
  133.5 8.4 %collective-permute-start.10 = (bf16[512,128]{1,0:T(8,128)(2,1)S(1)}, bf16[512,128]{1,0:T(8,128)(2,1)S(1)}, u32[]{:S(2)}, u32[]{:S(2)}) collective-permute-start(bf16[512,128]{1,0:T(8,128)(2,1)S(1)} %maximum_select_fusion.18), channel_id=1, source_target_pairs={{0,16},{16,0},{8,24},{24,8},{32,48},{48,32},{40,56},{56,40},{64,80... | collective-permute-start | bytes 393224 | tf_op jit(solution)/shard_map/ppermute | solution.py:16
  142.0 8.4 %collective-permute-start.11 = (bf16[1024,128]{1,0:T(8,128)(2,1)S(1)}, bf16[1024,128]{1,0:T(8,128)(2,1)}, u32[]{:S(2)}, u32[]{:S(2)}) collective-permute-start(bf16[1024,128]{1,0:T(8,128)(2,1)S(1)} %maximum_select_fusion.10), channel_id=1, source_target_pairs={{0,32},{32,0},{8,40},{40,8},{16,48},{48,16},{24,56},{56,24},{64,96... | collective-permute-start | bytes 786440 | tf_op jit(solution)/shard_map/ppermute | solution.py:16
  152.3 12.3 %collective-permute-start.12 = (f32[1024,128]{0,1:T(8,128)S(1)}, f32[1024,128]{0,1:T(8,128)S(1)}, u32[]{:S(2)}, u32[]{:S(2)}) collective-permute-start(f32[1024,128]{0,1:T(8,128)S(1)} %slice_select_fusion.1), channel_id=1, source_target_pairs={{0,32},{32,0},{8,40},{40,8},{16,48},{48,16},{24,56},{56,24},{64,96... | collective-permute-start | bytes 1572872 | tf_op jit(solution)/shard_map/ppermute | solution.py:16
  164.7 10.6 %collective-permute-start.13 = (f32[512,128]{0,1:T(8,128)S(1)}, f32[512,128]{0,1:T(8,128)S(1)}, u32[]{:S(2)}, u32[]{:S(2)}) collective-permute-start(f32[512,128]{0,1:T(8,128)S(1)} %slice_select_fusion.5), channel_id=1, source_target_pairs={{0,16},{16,0},{8,24},{24,8},{32,48},{48,32},{40,56},{56,40},{64,80... | collective-permute-start | bytes 786440 | tf_op jit(solution)/shard_map/ppermute | solution.py:16
  175.4 6.9 %collective-permute-start.14 = (f32[256,128]{0,1:T(8,128)S(1)}, f32[256,128]{0,1:T(8,128)S(1)}, u32[]{:S(2)}, u32[]{:S(2)}) collective-permute-start(f32[256,128]{0,1:T(8,128)S(1)} %slice_select_fusion.11), channel_id=1, source_target_pairs={{0,8},{8,0},{16,24},{24,16},{32,40},{40,32},{48,56},{56,48},{64,72... | collective-permute-start | bytes 393224 | tf_op jit(solution)/shard_map/ppermute | solution.py:16
  183.0 113.9 %reduce-scatter.21.cloned.1.call-start = ((), (), s32[]{:S(2)}) async-start(), calls=%async_computation.13 | async-start | bytes 147456 | tf_op jit(solution)/shard_map/reduce_scatter | solution.py:51
  224.6 13.0 %collective-permute-start.15 = (f32[1024,128]{0,1:T(8,128)S(1)}, f32[1024,128]{0,1:T(8,128)S(1)}, u32[]{:S(2)}, u32[]{:S(2)}) collective-permute-start(f32[1024,128]{0,1:T(8,128)S(1)} %slice_select_fusion), channel_id=1, source_target_pairs={{0,32},{32,0},{8,40},{40,8},{16,48},{48,16},{24,56},{56,24},{64,96... | collective-permute-start | bytes 1572872 | tf_op jit(solution)/shard_map/ppermute | solution.py:16
  237.8 9.8 %collective-permute-start.16 = (f32[512,128]{0,1:T(8,128)S(1)}, f32[512,128]{0,1:T(8,128)S(1)}, u32[]{:S(2)}, u32[]{:S(2)}) collective-permute-start(f32[512,128]{0,1:T(8,128)S(1)} %slice_select_fusion.4), channel_id=1, source_target_pairs={{0,16},{16,0},{8,24},{24,8},{32,48},{48,32},{40,56},{56,40},{64,80... | collective-permute-start | bytes 786440 | tf_op jit(solution)/shard_map/ppermute | solution.py:16
  247.6 6.9 %collective-permute-start.17 = (f32[256,128]{0,1:T(8,128)S(1)}, f32[256,128]{0,1:T(8,128)S(1)}, u32[]{:S(2)}, u32[]{:S(2)}) collective-permute-start(f32[256,128]{0,1:T(8,128)S(1)} %slice_select_fusion.10), channel_id=1, source_target_pairs={{0,8},{8,0},{16,24},{24,16},{32,40},{40,32},{48,56},{56,48},{64,72... | collective-permute-start | bytes 393224 | tf_op jit(solution)/shard_map/ppermute | solution.py:16
  255.3 99.6 %reduce-scatter.23.cloned.1.call-start = ((), (), s32[]{:S(2)}) async-start(), calls=%async_computation.14 | async-start | bytes 147456
  298.1 9.8 %collective-permute-start.18 = (f32[512,128]{0,1:T(8,128)S(1)}, f32[512,128]{0,1:T(8,128)S(1)}, u32[]{:S(2)}, u32[]{:S(2)}) collective-permute-start(f32[512,128]{0,1:T(8,128)S(1)} %slice_select_fusion.3), channel_id=1, source_target_pairs={{0,16},{16,0},{8,24},{24,8},{32,48},{48,32},{40,56},{56,40},{64,80... | collective-permute-start | bytes 786440 | tf_op jit(solution)/shard_map/ppermute | solution.py:16
  307.9 6.9 %collective-permute-start.19 = (f32[256,128]{0,1:T(8,128)S(1)}, f32[256,128]{0,1:T(8,128)S(1)}, u32[]{:S(2)}, u32[]{:S(2)}) collective-permute-start(f32[256,128]{0,1:T(8,128)S(1)} %slice_select_fusion.9), channel_id=1, source_target_pairs={{0,8},{8,0},{16,24},{24,16},{32,40},{40,32},{48,56},{56,48},{64,72... | collective-permute-start | bytes 393224 | tf_op jit(solution)/shard_map/ppermute | solution.py:16
  315.6 97.5 %reduce-scatter.25.cloned.1.call-start = ((), (), s32[]{:S(2)}) async-start(), calls=%async_computation.15 | async-start | bytes 147456 | tf_op jit(solution)/shard_map/reduce_scatter | solution.py:51
  356.0 9.9 %collective-permute-start.20 = (f32[512,128]{0,1:T(8,128)S(1)}, f32[512,128]{0,1:T(8,128)S(1)}, u32[]{:S(2)}, u32[]{:S(2)}) collective-permute-start(f32[512,128]{0,1:T(8,128)S(1)} %slice_select_fusion.2), channel_id=1, source_target_pairs={{0,16},{16,0},{8,24},{24,8},{32,48},{48,32},{40,56},{56,40},{64,80... | collective-permute-start | bytes 786440 | tf_op jit(solution)/shard_map/ppermute | solution.py:16
  366.0 6.9 %collective-permute-start.21 = (f32[256,128]{0,1:T(8,128)S(1)}, f32[256,128]{0,1:T(8,128)S(1)}, u32[]{:S(2)}, u32[]{:S(2)}) collective-permute-start(f32[256,128]{0,1:T(8,128)S(1)} %slice_select_fusion.8), channel_id=1, source_target_pairs={{0,8},{8,0},{16,24},{24,16},{32,40},{40,32},{48,56},{56,48},{64,72... | collective-permute-start | bytes 393224 | tf_op jit(solution)/shard_map/ppermute | solution.py:16
  373.7 85.5 %reduce-scatter.27.cloned.1.call-start = ((), (), s32[]{:S(2)}) async-start(), calls=%async_computation.16 | async-start | bytes 147456
  414.2 6.9 %collective-permute-start.22 = (f32[256,128]{0,1:T(8,128)S(1)}, f32[256,128]{0,1:T(8,128)S(1)}, u32[]{:S(2)}, u32[]{:S(2)}) collective-permute-start(f32[256,128]{0,1:T(8,128)S(1)} %slice_select_fusion.7), channel_id=1, source_target_pairs={{0,8},{8,0},{16,24},{24,16},{32,40},{40,32},{48,56},{56,48},{64,72... | collective-permute-start | bytes 393224 | tf_op jit(solution)/shard_map/ppermute | solution.py:16
  421.8 83.6 %reduce-scatter.29.cloned.1.call-start = ((), (), s32[]{:S(2)}) async-start(), calls=%async_computation.17 | async-start | bytes 147456
  460.2 6.9 %collective-permute-start.23 = (f32[256,128]{0,1:T(8,128)S(1)}, f32[256,128]{0,1:T(8,128)S(1)}, u32[]{:S(2)}, u32[]{:S(2)}) collective-permute-start(f32[256,128]{0,1:T(8,128)S(1)} %slice_select_fusion.6), channel_id=1, source_target_pairs={{0,8},{8,0},{16,24},{24,16},{32,40},{40,32},{48,56},{56,48},{64,72... | collective-permute-start | bytes 393224 | tf_op jit(solution)/shard_map/ppermute | solution.py:16
  (15 other events, 399.8 us)
Sparse Core Ops, SparseCore 0:
  183.1 40.2 reduce-scatter.18
  255.4 41.4 reduce-scatter.20
  315.7 39.1 reduce-scatter.22
  373.8 39.3 reduce-scatter.24
  421.9 37.1 reduce-scatter.26
  468.0 37.4 reduce-scatter.28
